TPU v7x, 32 devices: a whole 2x2x4 slice. The times are simulated.
32 devices in a mesh: rows: 8 (over z, x), feat: 4 (over y, core).
Axes of the slice: x: 2, y: 2, z: 4, core: 2. Of those that a mesh axis runs over, the one named last changes fastest.
Arguments:
- bins: int32 [256, 12288], P('feat', 'rows'), may hold values from 0 to 255
- gradients: bfloat16 [12288], P('rows'), may hold values from -11 to 14
- hessians: bfloat16 [12288], P('rows'), may hold values from 0.099609375 to 1
- predictions: float32 [12288], P('rows'), may hold values from -6 to 6
- leaf: int32 [12288], P('rows'), may hold values from 0 to 7
- split_feature: int32 [8], replicated, may hold values from 0 to 255
- split_bin: int32 [8], replicated, may hold values from 0 to 254
- row_counts: int32 [8], P('rows'), may hold values from 96 to 1536, as said below
Outputs:
- hist: float32 [4, 64, 2, 16, 256], P('feat', 'rows')
- new_leaf: int32 [12288], P('rows')
- new_pred: float32 [12288], P('rows')
Inputs may be any that keep to these rules, and one draw needn't show every extreme that they name: `row_counts`: some sweep batch has all 1536 rows live.
All inputs are finite; a program needn't handle non-finite values.
Results may differ from a plain program's by a relative error of at most 0.0003.
Values may be sent and summed in bfloat16 or wider, within the bound.
A program may use at most 128 MiB of HBM per device.

v0:
```python
import math

import jax
import jax.numpy as jnp
from jax import lax
from jax.sharding import PartitionSpec as P

B = 256
LEAVES = 8


def build_terms(columns, weights, blocks, blocking):
    width = columns.shape[0]
    kinds = weights.shape[0]
    levels = jnp.arange(B, dtype=jnp.int32)
    flipped = columns.T

    def add_block(step, accum):
        start = step * blocking
        cells = lax.dynamic_slice_in_dim(flipped, start, blocking, 0)
        wrows = lax.dynamic_slice_in_dim(weights, start, blocking, 1)
        table = (cells[:, :, None] == levels[None, None, :]).astype(jnp.bfloat16)
        table = table.reshape(blocking, width * B)
        return accum + jnp.dot(wrows, table, preferred_element_type=jnp.float32)

    accum = lax.fori_loop(0, blocks, add_block, jnp.zeros((kinds, width * B), jnp.float32))
    return accum.reshape(2, kinds // 2, width, B).transpose(2, 0, 1, 3)


def make_weights(member, grad_live, hess_live):
    zero = jnp.zeros((), jnp.bfloat16)
    upper = jnp.where(member, grad_live[None, :], zero)
    lower = jnp.where(member, hess_live[None, :], zero)
    return jnp.concatenate([upper, lower], 0)


def body(bins, gradients, hessians, predictions, leaf, split_feature, split_bin, row_counts):
    width, rows_here = bins.shape
    kids = 2 * LEAVES
    offset = lax.axis_index("feat") * width
    slots = jnp.arange(LEAVES, dtype=jnp.int32)
    match = leaf[:, None] == slots[None, :]
    wanted = jnp.sum(jnp.where(match, split_feature[None, :], 0), 1)
    cutoff = jnp.sum(jnp.where(match, split_bin[None, :], 0), 1)
    local = wanted - offset
    owned = (local >= 0) & (local < width)
    feature_ids = jnp.arange(width, dtype=jnp.int32)
    picked = feature_ids[:, None] == local[None, :]
    chosen = jnp.sum(jnp.where(picked, bins, 0), 0)
    flags = jnp.where(owned & (chosen > cutoff), 1.0, 0.0).astype(jnp.bfloat16)
    every = lax.all_gather(flags, "feat", axis=0, tiled=True).reshape(-1, rows_here)
    merged = jnp.sum(every.astype(jnp.float32), 0)
    going = jnp.where(merged > 0.5, 1, 0).astype(jnp.int32)
    new_leaf = 2 * leaf + going
    live = jnp.arange(rows_here, dtype=jnp.int32) < row_counts[0]
    zero = jnp.zeros((), jnp.bfloat16)
    grad_live = jnp.where(live, gradients, zero)
    hess_live = jnp.where(live, hessians, zero)
    kid_slots = jnp.arange(kids, dtype=jnp.int32)
    member = new_leaf[None, :] == kid_slots[:, None]
    weights = make_weights(member, grad_live, hess_live)
    blocking = math.gcd(rows_here, 512)
    blocks = rows_here // blocking
    hist = lax.psum_scatter(
        build_terms(bins, weights, blocks, blocking), "rows", scatter_dimension=0, tiled=True
    )
    paired = jnp.stack([grad_live.astype(jnp.float32), hess_live.astype(jnp.float32)], 0)
    partial_totals = jnp.einsum("cr,kr->kc", member.astype(jnp.float32), paired)
    totals = lax.psum(partial_totals, "rows")
    value = -totals[0] / (totals[1] + 1.0)
    gained = jnp.sum(jnp.where(member, value[:, None], jnp.float32(0.0)), 0)
    new_pred = predictions + 0.5 * gained
    return (hist[None], new_leaf, new_pred)


def solution(mesh):
    in_specs = (P("feat", "rows"), P("rows"), P("rows"), P("rows"), P("rows"), P(), P(), P("rows"))
    out_specs = (P("feat", "rows", None, None, None), P("rows"), P("rows"))
    return jax.shard_map(body, mesh=mesh, in_specs=in_specs, out_specs=out_specs, check_vma=False)
```

profile of v0, /device:TPU:0, one launch (start us, length us, event | category | flops | bytes accessed | tf_op | source)
XLA Modules:
  0.0 239.5 jit_solution(61274957074654994)
XLA Ops:
  7.2 1.3 copy.16
  8.5 0.8 select_reduce_fusion.2
  9.3 1.1 select_reduce_fusion
  10.4 6.2 %all-gather = bf16[4,1,1536]{2,1,0:T(2,128)(2,1)S(1)} all-gather(bf16[1,1,1536]{2,1,0:T(2,128)(2,1)S(1)} %reshape.49), channel_id=1, replica_groups=mesh['rows'=8,'feat'=4] {'feat'}, dimensions={0}, use_global_device_ids=true | all-gather | bytes 15360 | tf_op jit(solution)/shard_map/all_gather | solution.py:51
  16.7 0.7 select_add_fusion
  18.0 0.7 fusion.14
  18.8 0.5 copy-done.2
  19.3 137.9 %while.14 = (s32[]{:T(128)}, f32[32,16384]{1,0:T(8,128)}, bf16[32,1536]{1,0:T(8,128)(2,1)S(1)}, s32[1536,64]{1,0:T(8,128)S(1)}, s32[]{:T(128)}, /*index=5*/s32[]{:T(128)}, s32[]{:T(128)}, s32[]{:T(128)}) while((s32[]{:T(128)}, f32[32,16384]{1,0:T(8,128)}, bf16[32,1536]{1,0:T(8,128)(2,1)S(1)}, s32[1536,64]{1,0:T(8,128)S(1)}, ...), condition=%wide.region_5.6_spmd.clone, body=%wide.region_4.5_spmd.clone.sunk | while | flops 546308096 | bytes 139100320 | solution.py:26
  19.4 4.9 %eq.145 = s32[512,64,256]{2,1,0:T(8,128)S(1)} broadcast(s32[512,64]{1,0:T(8,128)S(1)} %constant_dynamic-slice_fusion.2), dimensions={0,1} | broadcast | bytes 33685504 | tf_op jit(solution)/shard_map/while/body/eval_jaxpr/eq | solution.py:22
  24.3 25.6 %copy.23 = s32[64,8,64,256]{3,1,2,0:T(8,128)} copy(s32[64,8,64,256]{3,2,1,0:T(8,128)S(1)} %bitcast.27) | data formatting | bytes 67108864 | tf_op jit(solution)/shard_map/while
  49.9 15.0 %fusion.24 = f32[32,16384]{1,0:T(8,128)} fusion(s32[512,16384]{1,0:T(8,128)} %bitcast.26, s32[16384]{0:T(1024)S(1)} %bitcast.30, f32[32,16384]{1,0:T(8,128)} %get-tuple-element.172, pred[]{:T(512)S(6)} %compare.3, bf16[32,1536]{1,0:T(8,128)(2,1)S(1)} %get-tuple-element.181, s32[]{:T(128)S(6)} %select_n.67), kind=kOutput, calls=%fused_computation.3.clone.1 | convolution fusion | flops 546308096 | bytes 37847044 | tf_op jit(solution)/shard_map/while/body/eval_jaxpr/dot_general | solution.py:24
  64.9 4.9 %eq.145 = s32[512,64,256]{2,1,0:T(8,128)S(1)} broadcast(s32[512,64]{1,0:T(8,128)S(1)} %constant_dynamic-slice_fusion.2), dimensions={0,1} | broadcast | bytes 33685504 | tf_op jit(solution)/shard_map/while/body/eval_jaxpr/eq | solution.py:22
  69.8 25.6 %copy.23 = s32[64,8,64,256]{3,1,2,0:T(8,128)} copy(s32[64,8,64,256]{3,2,1,0:T(8,128)S(1)} %bitcast.27) | data formatting | bytes 67108864 | tf_op jit(solution)/shard_map/while
  95.4 15.6 %fusion.24 = f32[32,16384]{1,0:T(8,128)} fusion(s32[512,16384]{1,0:T(8,128)} %bitcast.26, s32[16384]{0:T(1024)S(1)} %bitcast.30, f32[32,16384]{1,0:T(8,128)} %get-tuple-element.172, pred[]{:T(512)S(6)} %compare.3, bf16[32,1536]{1,0:T(8,128)(2,1)S(1)} %get-tuple-element.181, s32[]{:T(128)S(6)} %select_n.67), kind=kOutput, calls=%fused_computation.3.clone.1 | convolution fusion | flops 546308096 | bytes 37847044 | tf_op jit(solution)/shard_map/while/body/eval_jaxpr/dot_general | solution.py:24
  111.1 4.9 %eq.145 = s32[512,64,256]{2,1,0:T(8,128)S(1)} broadcast(s32[512,64]{1,0:T(8,128)S(1)} %constant_dynamic-slice_fusion.2), dimensions={0,1} | broadcast | bytes 33685504 | tf_op jit(solution)/shard_map/while/body/eval_jaxpr/eq | solution.py:22
  116.0 25.6 %copy.23 = s32[64,8,64,256]{3,1,2,0:T(8,128)} copy(s32[64,8,64,256]{3,2,1,0:T(8,128)S(1)} %bitcast.27) | data formatting | bytes 67108864 | tf_op jit(solution)/shard_map/while
  141.6 15.6 %fusion.24 = f32[32,16384]{1,0:T(8,128)} fusion(s32[512,16384]{1,0:T(8,128)} %bitcast.26, s32[16384]{0:T(1024)S(1)} %bitcast.30, f32[32,16384]{1,0:T(8,128)} %get-tuple-element.172, pred[]{:T(512)S(6)} %compare.3, bf16[32,1536]{1,0:T(8,128)(2,1)S(1)} %get-tuple-element.181, s32[]{:T(128)S(6)} %select_n.67), kind=kOutput, calls=%fused_computation.3.clone.1 | convolution fusion | flops 546308096 | bytes 37847044 | tf_op jit(solution)/shard_map/while/body/eval_jaxpr/dot_general | solution.py:24
  157.2 2.2 copy.20
  159.4 1.5 bitcast_bitcast_fusion
  161.0 0.7 copy-done.5
  161.8 22.1 %psum.7 = f32[2,16]{1,0:T(2,128)S(1)} all-reduce(f32[2,16]{1,0:T(2,128)S(1)} %fusion.10), channel_id=1, replica_groups=mesh['rows'=8,'feat'=4] {'rows'}, use_global_device_ids=true, to_apply=%region_7.8 | all-reduce | flops 32 | bytes 256 | tf_op jit(solution)/shard_map/psum | solution.py:69
  184.0 0.6 multiply_add_fusion
  184.7 46.3 %reduce-scatter.2.cloned.1.call-done = f32[8,2,16,256]{3,0,2,1:T(8,128)} async-done(((f32[64,2,16,256]{3,0,2,1:T(8,128)}), f32[8,2,16,256]{3,0,2,1:T(8,128)}) %reduce-scatter.2.cloned.1.call-update) | async-done | bytes 262160 | tf_op jit(solution)/shard_map/reduce_scatter | solution.py:64
  230.9 1.7 copy.17
  (35 shorter events, 0.6 us)
Async XLA Ops:
  7.2 223.8 %reduce-scatter.2.cloned.1.call-start = ((), (), s32[]{:S(2)}) async-start(), calls=%async_computation.1 | async-start | bytes 2359296 | tf_op jit(solution)/shard_map/reduce_scatter | solution.py:64
  17.4 1.4 copy-start
  18.7 0.6 copy-start.2
  18.7 0.6 copy-start.4
  160.9 0.7 copy-start.5
  160.9 0.7 copy-start.3
  160.9 0.7 copy-start.1
  160.9 23.1 %copy-start.6 = (f32[1536]{0:T(1024)S(1)}, f32[1536]{0:T(1024)}, u32[]{:S(2)}) copy-start(f32[1536]{0:T(1024)} %param.13) | copy-start | bytes 18436
Sparse Core Ops, SparseCore 0:
  161.1 69.8 reduce-scatter.1
where the time goes:
time: 240 us
  local copies, waits for them, and re-layouts  99.5 us (41%)
  matrix products  46.4 us (19%)
  waiting for transfers between devices  46.3 us (19%)
  blocking collectives  28.3 us (12%)
  between operations  14.8 us (6%)
  other arithmetic  4.06 us (2%)
    while x9, local copies, waits for them, and re-layouts  76.8 us
    reduce_scatter x1, waiting for transfers between devices, body(): lax.psum_scatter(build_terms(bins, weights, blocks, blocking), 'rows', sc...  46.3 us
    dot_general x3, matrix products, add_block(): return accum + jnp.dot(wrows, table, preferred_element_type=jnp.float32)  46.3 us
    psum x1, blocking collectives, body(): totals = lax.psum(partial_totals, 'rows')  22.1 us
    eq x3, local copies, waits for them, and re-layouts, add_block(): table = (cells[:, :, None] == levels[None, None, :]).astype(jnp.bfloat16)  14.7 us
    unnamed x18, local copies, waits for them, and re-layouts  6.46 us
    all_gather x1, blocking collectives, body(): lax.all_gather(flags, 'feat', axis=0, tiled=True).reshape(-1, rows_here)  6.22 us
  transfers between devices with their start and end apart: 1, of which 1 were waited for; matrix products, arithmetic and copies ran while one was open for 0% of the time, Pallas kernels for 0%

commit v1 on v0

v1 whole, which is shorter than its diff:
```python
import functools

import jax
import jax.numpy as jnp
from jax import lax
from jax.experimental import pallas as pl
from jax.experimental.pallas import tpu as pltpu
from jax.sharding import PartitionSpec as P

B = 256
LANES = 128
HALF = 128
STEP = 2
MESH = pl.DeviceIdType.MESH


def round_up(value, unit):
    return -(-value // unit) * unit


def pad_rows(x, rows):
    if x.shape[0] == rows:
        return x
    return jnp.concatenate([x, jnp.zeros((rows - x.shape[0], x.shape[1]), x.dtype)], 0)


def exchange_kernel(dims, bins_ref, grad_ref, hess_ref, leaf_ref, feature_ref, bin_ref, count_ref,
                    early_ref, late_ref, out_early, out_late, flag_in,
                    flag_send, flag_recv, early_send, early_recv, late_send, late_recv):
    n_rows, n_feat, owned, padded, chunks, leaves = dims
    width = owned * n_rows
    me_r = lax.axis_index("rows")
    me_f = lax.axis_index("feat")
    small = late_ref.shape[1]
    cells = chunks * padded

    def row_peer(step):
        return lax.rem(me_r + step, n_rows)

    def feat_peer(step):
        return lax.rem(me_f + step, n_feat)

    barrier = pltpu.get_barrier_semaphore()
    for step in range(1, n_feat):
        pl.semaphore_signal(barrier, inc=1, device_id=(me_r, feat_peer(step)), device_id_type=MESH)
    for step in range(1, n_rows):
        pl.semaphore_signal(barrier, inc=1, device_id=(row_peer(step), me_f), device_id_type=MESH)

    leaf = leaf_ref[...]
    wanted = jnp.zeros(leaf.shape, jnp.int32)
    cutoff = jnp.zeros(leaf.shape, jnp.int32)
    for slot in range(leaves):
        here = leaf == slot
        wanted = jnp.where(here, feature_ref[slot], wanted)
        cutoff = jnp.where(here, bin_ref[slot], cutoff)
    local = wanted - me_f * width
    ids = lax.broadcasted_iota(jnp.int32, (width, LANES), 0)
    chosen = []
    for chunk in range(chunks):
        block = bins_ref[:, chunk * LANES:(chunk + 1) * LANES]
        hit = ids == local[chunk:chunk + 1, :]
        chosen.append(jnp.sum(jnp.where(hit, block.astype(jnp.float32), 0.0), 0, keepdims=True))
    chosen = jnp.concatenate(chosen, 0)
    mine = (local >= 0) & (local < width)
    flags = jnp.where(mine & (chosen > cutoff.astype(jnp.float32)), 1.0, 0.0)
    flag_in[me_f] = pad_rows(flags, small).astype(jnp.bfloat16)

    pl.semaphore_wait(barrier, n_feat - 1 + n_rows - 1)
    flag_copies = []
    for step in range(1, n_feat):
        copy = pltpu.make_async_remote_copy(
            src_ref=flag_in.at[me_f], dst_ref=flag_in.at[me_f],
            send_sem=flag_send.at[step - 1], recv_sem=flag_recv.at[step - 1],
            device_id=(me_r, feat_peer(step)), device_id_type=MESH)
        copy.start()
        flag_copies.append(copy)

    count = count_ref[0]
    spot = (lax.broadcasted_iota(jnp.int32, leaf.shape, 0) * LANES
            + lax.broadcasted_iota(jnp.int32, leaf.shape, 1))
    live = spot < count
    upper = jnp.full((1, LANES), count // 8, jnp.int32).astype(jnp.float32)
    lower = jnp.full((1, LANES), count % 8, jnp.int32).astype(jnp.float32)
    grad = jnp.where(live, grad_ref[...].astype(jnp.float32), 0.0)
    hess = jnp.where(live, hess_ref[...].astype(jnp.float32), 0.0)
    tail = jnp.concatenate([pad_rows(jnp.concatenate([grad, upper, lower], 0), small),
                            pad_rows(hess, small)], 0).astype(jnp.bfloat16)
    for target in range(n_rows):
        blocks = []
        for chunk in range(chunks):
            block = bins_ref[target * owned:(target + 1) * owned, chunk * LANES:(chunk + 1) * LANES]
            blocks.append(pad_rows(block.astype(jnp.float32), padded))
        packed = jnp.concatenate(blocks, 0)
        out_early[target, :cells, :] = pad_rows(packed, cells).astype(jnp.bfloat16)
        out_early[target, cells:, :] = tail
    early_copies = []
    for step in range(1, n_rows):
        copy = pltpu.make_async_remote_copy(
            src_ref=out_early.at[row_peer(step)], dst_ref=early_ref.at[me_r],
            send_sem=early_send.at[step - 1], recv_sem=early_recv.at[step - 1],
            device_id=(row_peer(step), me_f), device_id_type=MESH)
        copy.start()
        early_copies.append(copy)

    for copy in flag_copies:
        copy.wait()
    merged = jnp.zeros((small, LANES), jnp.float32)
    for slot in range(n_feat):
        merged = merged + flag_in[slot].astype(jnp.float32)
    going = jnp.where(merged > 0.5, 1.0, 0.0)
    child = 2.0 * pad_rows(leaf.astype(jnp.float32), small) + going
    out_late[...] = child.astype(jnp.bfloat16)
    late_copies = []
    for step in range(1, n_rows):
        copy = pltpu.make_async_remote_copy(
            src_ref=out_late, dst_ref=late_ref.at[me_r],
            send_sem=late_send.at[step - 1], recv_sem=late_recv.at[step - 1],
            device_id=(row_peer(step), me_f), device_id_type=MESH)
        copy.start()
        late_copies.append(copy)
    late_ref[me_r] = child.astype(jnp.bfloat16)
    early_ref[me_r] = out_early[me_r]
    for copy in early_copies + late_copies:
        copy.wait()


def histogram_kernel(dims, early_ref, late_ref, pred_ref, hist_ref, leaf_ref, new_ref, sums, tot):
    n_rows, owned, padded, chunks, kids = dims
    cells = chunks * padded
    small = late_ref.shape[1]
    sums[...] = jnp.zeros_like(sums)
    tot[...] = jnp.zeros_like(tot)
    levels = lax.broadcasted_iota(jnp.int32, (HALF, LANES), 0).astype(jnp.float32).astype(jnp.bfloat16)
    slots = lax.broadcasted_iota(jnp.int32, (kids, LANES), 0).astype(jnp.float32).astype(jnp.bfloat16)
    one = jnp.ones((), jnp.bfloat16)
    zero = jnp.zeros((), jnp.bfloat16)
    steps = []
    for batch in range(n_rows):
        held = early_ref[batch, cells:cells + small, :].astype(jnp.float32)
        count = held[chunks:chunks + 1, :] * 8.0 + held[chunks + 1:chunks + 2, :]
        count = jnp.max(count).astype(jnp.int32)
        steps.append((count + STEP * LANES - 1) // (STEP * LANES))

    for batch in range(n_rows):
        grads = early_ref[batch, cells:cells + small, :].astype(jnp.float32)
        def one_step(step, carry, batch=batch):
            start = pl.multiple_of(step * STEP * padded, STEP * padded)
            block = early_ref[batch, pl.ds(start, STEP * padded), :].astype(jnp.float32)
            high = jnp.where(block >= float(HALF), 1.0, 0.0)
            low = block - high * float(HALF)
            weights = []
            for part in range(STEP):
                chunk = step * STEP + part
                pick = lax.broadcasted_iota(jnp.int32, (small, LANES), 0) == chunk
                def row(ref_value):
                    return jnp.sum(jnp.where(pick, ref_value.astype(jnp.float32), 0.0), 0, keepdims=True).astype(jnp.bfloat16)
                child = row(late_ref[batch])
                grad = row(early_ref[batch, cells:cells + small, :])
                hess = row(early_ref[batch, cells + small:cells + 2 * small, :])
                member = slots == child
                weights.append(jnp.concatenate([jnp.where(member, grad, zero), jnp.where(member, hess, zero)], 0))
            tot[...] += sum(w.astype(jnp.float32) for w in weights)
            both = jnp.concatenate(weights, 1)
            for f in range(owned):
                hot = []
                top = []
                for part in range(STEP):
                    at = part * padded + f
                    hot.append(jnp.where(levels == low[at:at + 1, :].astype(jnp.bfloat16), one, zero))
                    top.append(jnp.broadcast_to(high[at:at + 1, :], weights[0].shape).astype(jnp.bfloat16))
                hot = jnp.concatenate(hot, 1)
                upper = both * jnp.concatenate(top, 1)
                masked = jnp.concatenate([both - upper, upper], 0)
                sums[f] += lax.dot_general(masked, hot, (((1,), (1,)), ((), ())),
                                           preferred_element_type=jnp.float32)
            return carry
        lax.fori_loop(0, steps[batch], one_step, 0)

    for f in range(owned):
        hist_ref[f, :, :HALF] = sums[f, :2 * kids, :]
        hist_ref[f, :, HALF:] = sums[f, 2 * kids:, :]
    totals = jnp.sum(tot[...], 1, keepdims=True)
    value = -totals[:kids] / (totals[kids:] + 1.0)
    me_r = lax.axis_index("rows")
    child = late_ref[me_r].astype(jnp.float32)[:chunks]
    gained = jnp.zeros(child.shape, jnp.float32)
    for kid in range(kids):
        gained = jnp.where(child == float(kid), value[kid:kid + 1, :], gained)
    leaf_ref[...] = child.astype(jnp.int32)
    new_ref[...] = pred_ref[...] + 0.5 * gained


def solution(mesh):
    n_rows, n_feat = mesh.shape["rows"], mesh.shape["feat"]
    in_specs = (P("feat", "rows"), P("rows"), P("rows"), P("rows"), P("rows"), P(), P(), P("rows"))
    out_specs = (P("feat", "rows", None, None, None), P("rows"), P("rows"))
    vmem = pl.BlockSpec(memory_space=pltpu.VMEM)
    smem = pl.BlockSpec(memory_space=pltpu.SMEM)

    def body(bins, gradients, hessians, predictions, leaf, split_feature, split_bin, row_counts):
        width, rows_here = bins.shape
        leaves = split_feature.shape[0]
        kids = 2 * leaves
        owned = width // n_rows
        padded = round_up(owned, 8)
        chunks = rows_here // LANES
        small = round_up(chunks + 2, 16)
        cells = chunks * padded
        length = cells + 2 * small
        tall = (chunks, LANES)
        bf16 = jnp.bfloat16
        early, late = pl.pallas_call(
            functools.partial(exchange_kernel, (n_rows, n_feat, owned, padded, chunks, leaves)),
            out_shape=(jax.ShapeDtypeStruct((n_rows, length, LANES), bf16),
                       jax.ShapeDtypeStruct((n_rows, small, LANES), bf16)),
            in_specs=[vmem, vmem, vmem, vmem, smem, smem, smem],
            out_specs=(vmem, vmem),
            scratch_shapes=[
                pltpu.VMEM((n_rows, length, LANES), bf16),
                pltpu.VMEM((small, LANES), bf16),
                pltpu.VMEM((n_feat, small, LANES), bf16),
                pltpu.SemaphoreType.DMA((n_feat - 1,)),
                pltpu.SemaphoreType.DMA((n_feat - 1,)),
                pltpu.SemaphoreType.DMA((n_rows - 1,)),
                pltpu.SemaphoreType.DMA((n_rows - 1,)),
                pltpu.SemaphoreType.DMA((n_rows - 1,)),
                pltpu.SemaphoreType.DMA((n_rows - 1,)),
            ],
            compiler_params=pltpu.CompilerParams(collective_id=0, has_side_effects=True),
            name="exchange_rows",
        )(bins, gradients.reshape(tall), hessians.reshape(tall), leaf.reshape(tall),
          split_feature, split_bin, row_counts)
        hist, new_leaf, new_pred = pl.pallas_call(
            functools.partial(histogram_kernel, (n_rows, owned, padded, chunks, kids)),
            out_shape=(jax.ShapeDtypeStruct((owned, 2 * kids, B), jnp.float32),
                       jax.ShapeDtypeStruct(tall, jnp.int32),
                       jax.ShapeDtypeStruct(tall, jnp.float32)),
            in_specs=[vmem, vmem, vmem],
            out_specs=(vmem, vmem, vmem),
            scratch_shapes=[pltpu.VMEM((owned, 4 * kids, HALF), jnp.float32),
                            pltpu.VMEM((2 * kids, LANES), jnp.float32)],
            name="child_histograms",
        )(early, late, predictions.reshape(tall))
        return (hist.reshape(1, owned, 2, kids, B), new_leaf.reshape(rows_here), new_pred.reshape(rows_here))

    return jax.shard_map(body, mesh=mesh, in_specs=in_specs, out_specs=out_specs, check_vma=False)
```

time: 240 us -> 27.9 us (0.12)
  local copies, waits for them, and re-layouts: 99.5 us -> 0 us
  matrix products: 46.4 us -> 0 us
  waiting for transfers between devices: 46.3 us -> 0 us
  blocking collectives: 28.3 us -> 0 us
  Pallas kernels: 0 us -> 26.6 us
  between operations: 14.8 us -> 1.29 us
  other arithmetic: 4.06 us -> 0 us
    while x9 -> x0, local copies, waits for them, and re-layouts: 76.8 us -> none
    dot_general x4 -> x0, matrix products: 46.4 us -> none  [the longest x3 46.3 us: add_block(): return accum + jnp.dot(wrows, table, preferred_element_type=jnp.float32)]
    reduce_scatter x1 -> x0, waiting for transfers between devices: 46.3 us -> none  [body(): lax.psum_scatter(build_terms(bins, weights, blocks, blocking), 'rows', sc...]
    pallas_call x0 -> x2, Pallas kernels: none -> 26.6 us  [the longest x1 15.8 us: body(): pl.pallas_call(functools.partial(exchange_kernel, (n_rows, n_feat, owned,...]
    psum x1 -> x0, blocking collectives: 22.1 us -> none  [body(): totals = lax.psum(partial_totals, 'rows')]
    eq x3 -> x0, local copies, waits for them, and re-layouts: 14.7 us -> none  [add_block(): table = (cells[:, :, None] == levels[None, None, :]).astype(jnp.bfloat16)]
    unnamed x18 -> x0, local copies, waits for them, and re-layouts: 6.46 us -> none
    all_gather x1 -> x0, blocking collectives: 6.22 us -> none  [body(): lax.all_gather(flags, 'feat', axis=0, tiled=True).reshape(-1, rows_here)]
  transfers between devices with their start and end apart: 1 -> 0, of which waited for: 1 -> 0; matrix products, arithmetic and copies ran while one was open for 0% -> 0% of each run, Pallas kernels for 0% -> 0%
where the time goes in v1:
time: 27.9 us
  Pallas kernels  26.6 us (95%)
  between operations  1.29 us (5%)
    pallas_call x1, Pallas kernels, body(): pl.pallas_call(functools.partial(exchange_kernel, (n_rows, n_feat, owned,...  15.8 us
    pallas_call x1, Pallas kernels, body(): pl.pallas_call(functools.partial(histogram_kernel, (n_rows, owned, padded...  10.8 us

profile of v1, /device:TPU:0, one launch (start us, length us, event | category | flops | bytes accessed | tf_op | source)
XLA Modules:
  0.0 27.9 jit_solution(1583539048281956765)
XLA Ops:
  1.3 15.8 %exchange_rows.1 = (bf16[8,128,128]{2,1,0:T(8,128)(2,1)}, bf16[8,16,128]{2,1,0:T(8,128)(2,1)}) custom-call(s32[64,1536]{1,0:T(8,128)} %bins_ref.1, bf16[12,128]{1,0:T(8,128)(2,1)} %bitcast.9, bf16[12,128]{1,0:T(8,128)(2,1)} %bitcast.10, s32[12,128]{1,0:T(8,128)} %bitcast.7, s32[8]{0:T(128)} %feature_ref.1, s32[8]{0:T(128)} %bin_ref.1, s32[1]{0:T(128)S(6)} %copy.11.count_ref), custom_call_target="tpu_custom_call" | custom-call | tf_op jit(solution)/shard_map/exchange_rows/pallas_call | solution.py:212
  17.1 10.8 %child_histograms.1 = (f32[8,32,256]{2,1,0:T(8,128)}, s32[12,128]{1,0:T(8,128)}, f32[12,128]{1,0:T(8,128)}) custom-call(bf16[8,128,128]{2,1,0:T(8,128)(2,1)} %get-tuple-element.8.early_ref, bf16[8,16,128]{2,1,0:T(8,128)(2,1)} %get-tuple-element.9.late_ref, f32[12,128]{1,0:T(8,128)} %bitcast.8), custom_call_target="tpu_custom_call" | custom-call | tf_op jit(solution)/shard_map/child_histograms/pallas_call | solution.py:233

commit v2 on v1

--- a/solution.py
+++ b/solution.py
@@ -10,7 +10,10 @@
 B = 256
 LANES = 128
 HALF = 128
-STEP = 2
+TILE = 16
+PAIR = 2
+GROUP = 4
+VMEM_BYTES = 16 * 1024 * 1024
 MESH = pl.DeviceIdType.MESH
 
 
@@ -24,9 +27,9 @@
     return jnp.concatenate([x, jnp.zeros((rows - x.shape[0], x.shape[1]), x.dtype)], 0)
 
 
-def exchange_kernel(dims, bins_ref, grad_ref, hess_ref, leaf_ref, feature_ref, bin_ref, count_ref,
-                    early_ref, late_ref, out_early, out_late, flag_in,
-                    flag_send, flag_recv, early_send, early_recv, late_send, late_recv):
+def exchange_kernel(dims, bins_hbm, grad_ref, hess_ref, leaf_ref, feature_ref, bin_ref, count_ref,
+                    early_ref, late_ref, bins_ref, out_early, out_late, flag_in,
+                    bins_sem, flag_send, flag_recv, early_send, early_recv, late_send, late_recv):
     n_rows, n_feat, owned, padded, chunks, leaves = dims
     width = owned * n_rows
     me_r = lax.axis_index("rows")
@@ -40,6 +43,8 @@
     def feat_peer(step):
         return lax.rem(me_f + step, n_feat)
 
+    fetch = pltpu.make_async_copy(bins_hbm, bins_ref, bins_sem)
+    fetch.start()
     barrier = pltpu.get_barrier_semaphore()
     for step in range(1, n_feat):
         pl.semaphore_signal(barrier, inc=1, device_id=(me_r, feat_peer(step)), device_id_type=MESH)
@@ -54,6 +59,7 @@
         wanted = jnp.where(here, feature_ref[slot], wanted)
         cutoff = jnp.where(here, bin_ref[slot], cutoff)
     local = wanted - me_f * width
+    fetch.wait()
     ids = lax.broadcasted_iota(jnp.int32, (width, LANES), 0)
     chosen = []
     for chunk in range(chunks):
@@ -64,16 +70,6 @@
     mine = (local >= 0) & (local < width)
     flags = jnp.where(mine & (chosen > cutoff.astype(jnp.float32)), 1.0, 0.0)
     flag_in[me_f] = pad_rows(flags, small).astype(jnp.bfloat16)
-
-    pl.semaphore_wait(barrier, n_feat - 1 + n_rows - 1)
-    flag_copies = []
-    for step in range(1, n_feat):
-        copy = pltpu.make_async_remote_copy(
-            src_ref=flag_in.at[me_f], dst_ref=flag_in.at[me_f],
-            send_sem=flag_send.at[step - 1], recv_sem=flag_recv.at[step - 1],
-            device_id=(me_r, feat_peer(step)), device_id_type=MESH)
-        copy.start()
-        flag_copies.append(copy)
 
     count = count_ref[0]
     spot = (lax.broadcasted_iota(jnp.int32, leaf.shape, 0) * LANES
@@ -93,6 +89,15 @@
         packed = jnp.concatenate(blocks, 0)
         out_early[target, :cells, :] = pad_rows(packed, cells).astype(jnp.bfloat16)
         out_early[target, cells:, :] = tail
+    pl.semaphore_wait(barrier, n_feat - 1 + n_rows - 1)
+    flag_copies = []
+    for step in range(1, n_feat):
+        copy = pltpu.make_async_remote_copy(
+            src_ref=flag_in.at[me_f], dst_ref=flag_in.at[me_f],
+            send_sem=flag_send.at[step - 1], recv_sem=flag_recv.at[step - 1],
+            device_id=(me_r, feat_peer(step)), device_id_type=MESH)
+        copy.start()
+        flag_copies.append(copy)
     early_copies = []
     for step in range(1, n_rows):
         copy = pltpu.make_async_remote_copy(
@@ -124,65 +129,78 @@
         copy.wait()
 
 
-def histogram_kernel(dims, early_ref, late_ref, pred_ref, hist_ref, leaf_ref, new_ref, sums, tot):
+def histogram_kernel(dims, early_ref, late_ref, pred_ref, hist_ref, leaf_ref, new_ref, held, tot, order):
     n_rows, owned, padded, chunks, kids = dims
     cells = chunks * padded
     small = late_ref.shape[1]
-    sums[...] = jnp.zeros_like(sums)
+    bf16 = jnp.bfloat16
+    units = chunks // PAIR
+    hist_ref[...] = jnp.zeros_like(hist_ref)
     tot[...] = jnp.zeros_like(tot)
-    levels = lax.broadcasted_iota(jnp.int32, (HALF, LANES), 0).astype(jnp.float32).astype(jnp.bfloat16)
-    slots = lax.broadcasted_iota(jnp.int32, (kids, LANES), 0).astype(jnp.float32).astype(jnp.bfloat16)
-    one = jnp.ones((), jnp.bfloat16)
-    zero = jnp.zeros((), jnp.bfloat16)
-    steps = []
+    held[n_rows] = jnp.zeros(held.shape[1:], jnp.float32)
     for batch in range(n_rows):
-        held = early_ref[batch, cells:cells + small, :].astype(jnp.float32)
-        count = held[chunks:chunks + 1, :] * 8.0 + held[chunks + 1:chunks + 2, :]
+        held[batch, :2 * small, :] = early_ref[batch, cells:, :].astype(jnp.float32)
+        held[batch, 2 * small:, :] = late_ref[batch].astype(jnp.float32)
+    filled = jnp.int32(0)
+    for batch in range(n_rows):
+        count = held[batch, chunks:chunks + 1, :] * 8.0 + held[batch, chunks + 1:chunks + 2, :]
         count = jnp.max(count).astype(jnp.int32)
-        steps.append((count + STEP * LANES - 1) // (STEP * LANES))
-
-    for batch in range(n_rows):
-        grads = early_ref[batch, cells:cells + small, :].astype(jnp.float32)
-        def one_step(step, carry, batch=batch):
-            start = pl.multiple_of(step * STEP * padded, STEP * padded)
-            block = early_ref[batch, pl.ds(start, STEP * padded), :].astype(jnp.float32)
+        for unit in range(units):
+            order[filled] = batch * units + unit
+            filled = filled + jnp.where(count > unit * PAIR * LANES, 1, 0).astype(jnp.int32)
+    for extra in range(GROUP):
+        order[filled + extra] = n_rows * units
+
+    rows16 = lax.broadcasted_iota(jnp.int32, (TILE, LANES), 0).astype(jnp.float32)
+    levels = [(rows16 + float(TILE * at)).astype(bf16) for at in range(HALF // TILE)]
+    slots = lax.broadcasted_iota(jnp.int32, (kids, LANES), 0).astype(jnp.float32).astype(bf16)
+    one = jnp.ones((), bf16)
+    zero = jnp.zeros((), bf16)
+
+    def one_step(step, carry):
+        highs, lows, weights = [], [], []
+        for part in range(GROUP):
+            number = order[step * GROUP + part]
+            batch = number // units
+            unit = number - batch * units
+            source = jnp.minimum(batch, n_rows - 1)
+            start = pl.multiple_of(unit * PAIR * padded, PAIR * padded)
+            block = early_ref[source, pl.ds(start, PAIR * padded), :].astype(jnp.float32)
             high = jnp.where(block >= float(HALF), 1.0, 0.0)
             low = block - high * float(HALF)
-            weights = []
-            for part in range(STEP):
-                chunk = step * STEP + part
-                pick = lax.broadcasted_iota(jnp.int32, (small, LANES), 0) == chunk
-                def row(ref_value):
-                    return jnp.sum(jnp.where(pick, ref_value.astype(jnp.float32), 0.0), 0, keepdims=True).astype(jnp.bfloat16)
-                child = row(late_ref[batch])
-                grad = row(early_ref[batch, cells:cells + small, :])
-                hess = row(early_ref[batch, cells + small:cells + 2 * small, :])
+            for half in range(PAIR):
+                highs.append(high[half * padded:(half + 1) * padded])
+                lows.append(low[half * padded:(half + 1) * padded])
+                chunk = unit * PAIR + half
+                grad, hess, child = [
+                    jnp.broadcast_to(held[batch, pl.ds(chunk + small * kind, 1), :], (kids, LANES)).astype(bf16)
+                    for kind in range(3)]
                 member = slots == child
                 weights.append(jnp.concatenate([jnp.where(member, grad, zero), jnp.where(member, hess, zero)], 0))
-            tot[...] += sum(w.astype(jnp.float32) for w in weights)
-            both = jnp.concatenate(weights, 1)
-            for f in range(owned):
-                hot = []
-                top = []
-                for part in range(STEP):
-                    at = part * padded + f
-                    hot.append(jnp.where(levels == low[at:at + 1, :].astype(jnp.bfloat16), one, zero))
-                    top.append(jnp.broadcast_to(high[at:at + 1, :], weights[0].shape).astype(jnp.bfloat16))
-                hot = jnp.concatenate(hot, 1)
-                upper = both * jnp.concatenate(top, 1)
-                masked = jnp.concatenate([both - upper, upper], 0)
-                sums[f] += lax.dot_general(masked, hot, (((1,), (1,)), ((), ())),
-                                           preferred_element_type=jnp.float32)
-            return carry
-        lax.fori_loop(0, steps[batch], one_step, 0)
-
-    for f in range(owned):
-        hist_ref[f, :, :HALF] = sums[f, :2 * kids, :]
-        hist_ref[f, :, HALF:] = sums[f, 2 * kids:, :]
+        tot[...] += sum(w.astype(jnp.float32) for w in weights)
+        both = jnp.concatenate(weights, 1)
+        for f in range(owned):
+            hot = []
+            top = []
+            for high, low in zip(highs, lows):
+                level = jnp.broadcast_to(low[f:f + 1, :], (TILE, LANES)).astype(bf16)
+                hot.append(jnp.concatenate([jnp.where(level == at, one, zero) for at in levels], 0))
+                top.append(jnp.broadcast_to(high[f:f + 1, :], (2 * kids, LANES)).astype(bf16))
+            hot = jnp.concatenate(hot, 1)
+            upper = both * jnp.concatenate(top, 1)
+            masked = jnp.concatenate([both - upper, upper], 0)
+            found = lax.dot_general(masked, hot, (((1,), (1,)), ((), ())),
+                                    preferred_element_type=jnp.float32)
+            hist_ref[f, :, :HALF] += found[:2 * kids]
+            hist_ref[f, :, HALF:] += found[2 * kids:]
+        return carry
+
+    lax.fori_loop(0, (filled + GROUP - 1) // GROUP, one_step, 0)
+
     totals = jnp.sum(tot[...], 1, keepdims=True)
     value = -totals[:kids] / (totals[kids:] + 1.0)
     me_r = lax.axis_index("rows")
-    child = late_ref[me_r].astype(jnp.float32)[:chunks]
+    child = held[me_r, 2 * small:2 * small + chunks, :]
     gained = jnp.zeros(child.shape, jnp.float32)
     for kid in range(kids):
         gained = jnp.where(child == float(kid), value[kid:kid + 1, :], gained)
@@ -213,12 +231,14 @@
             functools.partial(exchange_kernel, (n_rows, n_feat, owned, padded, chunks, leaves)),
             out_shape=(jax.ShapeDtypeStruct((n_rows, length, LANES), bf16),
                        jax.ShapeDtypeStruct((n_rows, small, LANES), bf16)),
-            in_specs=[vmem, vmem, vmem, vmem, smem, smem, smem],
+            in_specs=[pl.BlockSpec(memory_space=pl.ANY), vmem, vmem, vmem, smem, smem, smem],
             out_specs=(vmem, vmem),
             scratch_shapes=[
+                pltpu.VMEM((width, rows_here), jnp.int32),
                 pltpu.VMEM((n_rows, length, LANES), bf16),
                 pltpu.VMEM((small, LANES), bf16),
                 pltpu.VMEM((n_feat, small, LANES), bf16),
+                pltpu.SemaphoreType.DMA,
                 pltpu.SemaphoreType.DMA((n_feat - 1,)),
                 pltpu.SemaphoreType.DMA((n_feat - 1,)),
                 pltpu.SemaphoreType.DMA((n_rows - 1,)),
@@ -226,7 +246,8 @@
                 pltpu.SemaphoreType.DMA((n_rows - 1,)),
                 pltpu.SemaphoreType.DMA((n_rows - 1,)),
             ],
-            compiler_params=pltpu.CompilerParams(collective_id=0, has_side_effects=True),
+            compiler_params=pltpu.CompilerParams(collective_id=0, has_side_effects=True,
+                                                 vmem_limit_bytes=VMEM_BYTES),
             name="exchange_rows",
         )(bins, gradients.reshape(tall), hessians.reshape(tall), leaf.reshape(tall),
           split_feature, split_bin, row_counts)
@@ -237,8 +258,10 @@
                        jax.ShapeDtypeStruct(tall, jnp.float32)),
             in_specs=[vmem, vmem, vmem],
             out_specs=(vmem, vmem, vmem),
-            scratch_shapes=[pltpu.VMEM((owned, 4 * kids, HALF), jnp.float32),
-                            pltpu.VMEM((2 * kids, LANES), jnp.float32)],
+            scratch_shapes=[pltpu.VMEM((n_rows + 1, 3 * small, LANES), jnp.float32),
+                            pltpu.VMEM((2 * kids, LANES), jnp.float32),
+                            pltpu.SMEM((n_rows * chunks // PAIR + GROUP,), jnp.int32)],
+            compiler_params=pltpu.CompilerParams(vmem_limit_bytes=VMEM_BYTES),
             name="child_histograms",
         )(early, late, predictions.reshape(tall))
         return (hist.reshape(1, owned, 2, kids, B), new_leaf.reshape(rows_here), new_pred.reshape(rows_here))

time: 27.9 us -> 25.9 us (0.928)
  Pallas kernels: 26.6 us -> 21.7 us
  local copies, waits for them, and re-layouts: 0 us -> 3.03 us
    pallas_call x1, Pallas kernels: 10.8 us -> 6.94 us  [body(): pl.pallas_call(functools.partial(histogram_kernel, (n_rows, owned, padded...]
    unnamed x0 -> x14, local copies, waits for them, and re-layouts: none -> 3.03 us
    pallas_call x1, Pallas kernels: 15.8 us -> 14.8 us  [body(): pl.pallas_call(functools.partial(exchange_kernel, (n_rows, n_feat, owned,...]
where the time goes in v2:
time: 25.9 us; the launch traced here: 26.1 us
  Pallas kernels  21.7 us (84%)
  local copies, waits for them, and re-layouts  3.03 us (12%)
  between operations  1.34 us (5%)
    pallas_call x1, Pallas kernels, body(): pl.pallas_call(functools.partial(exchange_kernel, (n_rows, n_feat, owned,...  14.8 us
    pallas_call x1, Pallas kernels, body(): pl.pallas_call(functools.partial(histogram_kernel, (n_rows, owned, padded...  6.94 us
    unnamed x14, local copies, waits for them, and re-layouts  3.03 us

profile of v2, /device:TPU:0, one launch (start us, length us, event | category | flops | bytes accessed | tf_op | source)
XLA Modules:
  0.0 26.1 jit_solution(7099855524532302337)
XLA Ops:
  0.6 0.0 copy-start.1
  1.3 0.0 copy-start.5
  1.3 0.0 copy-start.6
  1.3 0.0 copy-done.1
  1.3 0.6 %copy-done.5 = s32[8]{0:T(128)S(1)} copy-done((s32[8]{0:T(128)S(1)}, s32[8]{0:T(128)}, u32[]{:S(2)}) %copy-start.5) | copy-done | bytes 56
  2.0 0.0 copy-done.6
  2.0 0.0 copy-start
  2.0 1.0 %copy-done = s32[64,1536]{1,0:T(8,128)S(1)} copy-done((s32[64,1536]{1,0:T(8,128)S(1)}, s32[64,1536]{1,0:T(8,128)}, u32[]{:S(2)}) %copy-start) | copy-done | bytes 393240
  3.0 0.0 copy-start.3
  3.0 0.7 %copy-done.3 = bf16[1536]{0:T(1024)(128)(2,1)S(1)} copy-done((bf16[1536]{0:T(1024)(128)(2,1)S(1)}, bf16[1536]{0:T(1024)(128)(2,1)}, u32[]{:S(2)}) %copy-start.3) | copy-done | bytes 3096
  3.7 0.0 copy-start.4
  3.7 0.7 %copy-done.4 = bf16[1536]{0:T(1024)(128)(2,1)S(1)} copy-done((bf16[1536]{0:T(1024)(128)(2,1)S(1)}, bf16[1536]{0:T(1024)(128)(2,1)}, u32[]{:S(2)}) %copy-start.4) | copy-done | bytes 3096
  4.3 0.0 copy-start.2
  4.3 14.8 %exchange_rows.1 = (bf16[8,128,128]{2,1,0:T(8,128)(2,1)S(1)}, bf16[8,16,128]{2,1,0:T(8,128)(2,1)S(1)}) custom-call(s32[64,1536]{1,0:T(8,128)S(1)} %copy-done, bf16[12,128]{1,0:T(8,128)(2,1)S(1)} %bitcast.9, bf16[12,128]{1,0:T(8,128)(2,1)S(1)} %bitcast.10, s32[12,128]{1,0:T(8,128)S(1)} %bitcast.7, s32[8]{0:T(128)S(1)} %copy-done.5, s32[8]{0:T(128)S(1)} %copy-done.6, ...), custom_call_target="tpu_custom_call" | custom-call | tf_op jit(solution)/shard_map/exchange_rows/pallas_call | solution.py:230
  19.1 0.0 copy-done.2
  19.1 6.9 %child_histograms.1 = (f32[8,32,256]{2,1,0:T(8,128)}, s32[12,128]{1,0:T(8,128)}, f32[12,128]{1,0:T(8,128)}) custom-call(bf16[8,128,128]{2,1,0:T(8,128)(2,1)S(1)} %get-tuple-element.8.early_ref, bf16[8,16,128]{2,1,0:T(8,128)(2,1)S(1)} %get-tuple-element.9.late_ref, f32[12,128]{1,0:T(8,128)S(1)} %bitcast.8), custom_call_target="tpu_custom_call" | custom-call | tf_op jit(solution)/shard_map/child_histograms/pallas_call | solution.py:254
Async XLA Ops:
  0.6 0.7 %copy-start.1 = (s32[1536]{0:T(1024)S(1)}, s32[1536]{0:T(1024)}, u32[]{:S(2)}) copy-start(s32[1536]{0:T(1024)} %param.12) | copy-start | bytes 18436
  1.3 0.7 %copy-start.5 = (s32[8]{0:T(128)S(1)}, s32[8]{0:T(128)}, u32[]{:S(2)}) copy-start(s32[8]{0:T(128)} %feature_ref.1) | copy-start | bytes 100
  1.3 0.7 %copy-start.6 = (s32[8]{0:T(128)S(1)}, s32[8]{0:T(128)}, u32[]{:S(2)}) copy-start(s32[8]{0:T(128)} %bin_ref.1) | copy-start | bytes 100
  2.0 1.0 %copy-start = (s32[64,1536]{1,0:T(8,128)S(1)}, s32[64,1536]{1,0:T(8,128)}, u32[]{:S(2)}) copy-start(s32[64,1536]{1,0:T(8,128)} %bins_hbm.1) | copy-start | bytes 1179652
  3.0 0.7 %copy-start.3 = (bf16[1536]{0:T(1024)(128)(2,1)S(1)}, bf16[1536]{0:T(1024)(128)(2,1)}, u32[]{:S(2)}) copy-start(bf16[1536]{0:T(1024)(128)(2,1)} %param.9) | copy-start | bytes 9220
  3.7 0.7 %copy-start.4 = (bf16[1536]{0:T(1024)(128)(2,1)S(1)}, bf16[1536]{0:T(1024)(128)(2,1)}, u32[]{:S(2)}) copy-start(bf16[1536]{0:T(1024)(128)(2,1)} %param.10) | copy-start | bytes 9220
  4.3 14.8 %copy-start.2 = (f32[1536]{0:T(1024)S(1)}, f32[1536]{0:T(1024)}, u32[]{:S(2)}) copy-start(f32[1536]{0:T(1024)} %param.11) | copy-start | bytes 18436
